TPU v7x, 32 devices: a whole 2x2x4 slice. The times are simulated.
32 devices in a mesh: tm: 8 (over y, x, core), space: 4 (over z).
Axes of the slice: x: 2, y: 2, z: 4, core: 2. Of those that a mesh axis runs over, the one named last changes fastest.
Arguments:
- start: float32 [8, 2, 32, 64, 128], P('tm', None, 'space'), may hold values from -0.2 to 1.2
- conduct: float32 [32, 64, 128], P('space'), may hold values from 0.03 to 0.12
- threshold: float32 [32, 64, 128], P('space'), may hold values from 0.05 to 0.45
- recovery: float32 [32, 64, 128], P('space'), may hold values from 0.02 to 0.3
Outputs:
- final: float32 [8, 2, 32, 64, 128], P('tm', None, 'space')
All inputs are finite; a program needn't handle non-finite values.
Results may differ from a plain program's by a relative error of at most 0.0001.
Values sent between devices are 32-bit elements; how exact they have to be, the bound alone decides.
A program may use at most 64 MiB of HBM per device.

v0:
```python
import jax
import jax.numpy as jnp
from jax import lax
from jax.sharding import PartitionSpec as P

ITERS = 2


quad_first = (5.0 / 24.0, 1.0 / 3.0, -1.0 / 24.0)
quad_second = (-1.0 / 24.0, 1.0 / 3.0, 5.0 / 24.0)
node_step = 0.5
reaction = 2.0
recovery_ratio = 0.5


def extended(cells, sides, width):
    for axis, dim in sides:
        count = lax.axis_size(axis)
        ends = count - 1
        head = lax.slice_in_dim(cells, 0, width, axis=dim)
        tail = lax.slice_in_dim(cells, cells.shape[dim] - width, cells.shape[dim], axis=dim)
        cells = jnp.concatenate(
            [
                lax.ppermute(tail, axis, [(i, (i + 1) % count) for i in range(ends)]),
                cells,
                lax.ppermute(head, axis, [((i + 1) % count, i) for i in range(ends)]),
            ],
            axis=dim,
        )
    return cells


def passed_along(array, axis, by):
    count = lax.axis_size(axis)
    pairs = [(i, i + by) for i in range(count) if 0 <= i + by < count]
    return lax.ppermute(array, axis, pairs)


def quadrature(weights, terms):
    return weights[0] * terms[0] + weights[1] * terms[1] + weights[2] * terms[2]


def fine_laplace(padded, values):
    summed = padded[:, 2:, 1:-1, 1:-1] + padded[:, :-2, 1:-1, 1:-1]
    summed = summed + padded[:, 1:-1, 2:, 1:-1] + padded[:, 1:-1, :-2, 1:-1]
    summed = summed + padded[:, 1:-1, 1:-1, 2:] + padded[:, 1:-1, 1:-1, :-2]
    return summed - 6.0 * values


def coarse_laplace(padded, values):
    along_x = padded[:, 2:, 1:-1, 1:-1] + padded[:, :-2, 1:-1, 1:-1] - 2.0 * values
    along_y = padded[:, 1:-1, 2:, 1:-1] + padded[:, 1:-1, :-2, 1:-1] - 2.0 * values
    along_z = padded[:, 1:-1, 1:-1, 2:] + padded[:, 1:-1, 1:-1, :-2] - 2.0 * values
    return 0.25 * along_x + 0.25 * along_y + along_z


def forces(states, laplace, coeffs):
    conduct, threshold, recovery = coeffs
    excite = states[:, 0]
    slower = states[:, 1]
    driving = conduct * laplace + reaction * excite * (1.0 - excite) * (excite - threshold) - slower
    relaxing = recovery * (excite - recovery_ratio * slower)
    return jnp.stack([driving, relaxing], axis=1)


def restrict(values):
    sizes_of = values.shape
    blocks = values.reshape(
        sizes_of[:-3] + (sizes_of[-3] // 2, 2, sizes_of[-2] // 2, 2, sizes_of[-1])
    )
    return 0.25 * jnp.sum(blocks, axis=(-4, -2))


def prolong(values):
    sizes_of = values.shape
    widened = jnp.broadcast_to(
        values[..., :, None, :, None, :],
        sizes_of[:-3] + (sizes_of[-3], 2, sizes_of[-2], 2, sizes_of[-1]),
    )
    return widened.reshape(sizes_of[:-3] + (2 * sizes_of[-3], 2 * sizes_of[-2], sizes_of[-1]))


def side_pad(padded_x):
    return jnp.pad(padded_x, ((0, 0), (0, 0), (1, 1), (1, 1)))


def fine_single(state, coeffs):
    stacked = state[None]
    padded_x = extended(stacked[:, 0], (("space", 1),), 1)
    return forces(stacked, fine_laplace(side_pad(padded_x), stacked[:, 0]), coeffs)[0]


def per_device(start, conduct, threshold, recovery):
    fine_coeffs = (conduct, threshold, recovery)
    coarse_coeffs = (restrict(conduct), restrict(threshold), restrict(recovery))
    initial = start[0]
    start_terms = fine_single(initial, fine_coeffs)
    upper_nodes = jnp.stack([initial, initial])
    upper_terms = jnp.stack([start_terms, start_terms])
    old_first_terms = start_terms
    is_head = lax.axis_index("tm") == 0
    result = initial
    for sweep_index in range(ITERS):
        final_pass = sweep_index + 1 == ITERS
        if sweep_index == 0:
            term_zero = start_terms
        else:
            padded_x = extended(upper_nodes[:, 0], (("space", 1),), 1)
            upper_terms = forces(
                upper_nodes, fine_laplace(side_pad(padded_x), upper_nodes[:, 0]), fine_coeffs
            )
            term_zero = fine_single(initial, fine_coeffs)
        old_terms = (old_first_terms, upper_terms[0], upper_terms[1])
        node_one = (
            initial + node_step * (term_zero - old_terms[0]) + quadrature(quad_first, old_terms)
        )
        term_one = fine_single(node_one, fine_coeffs)
        node_two = (
            node_one + node_step * (term_one - old_terms[1]) + quadrature(quad_second, old_terms)
        )
        term_two = fine_single(node_two, fine_coeffs)
        new_terms = (term_zero, term_one, term_two)
        sum_first = quadrature(quad_first, new_terms)
        sum_second = quadrature(quad_second, new_terms)
        coarse_zero = restrict(initial)
        base_one = restrict(node_one)
        coarse_one = coarse_zero + restrict(sum_first)
        pair_states = jnp.stack([base_one, coarse_one])
        coarse_x = extended(pair_states[:, 0], (("space", 1),), 1)
        pair_terms = forces(
            pair_states, coarse_laplace(side_pad(coarse_x), pair_states[:, 0]), coarse_coeffs
        )
        coarse_two = coarse_one + node_step * (pair_terms[1] - pair_terms[0]) + restrict(sum_second)
        coarse_jump = coarse_two - restrict(node_two)
        node_two_new = node_two + prolong(coarse_jump)
        if final_pass:
            result = node_two_new
        else:
            node_one_new = node_one + prolong(coarse_one - base_one)
            received = passed_along(node_two_new, "tm", 1)
            upper_nodes = jnp.stack([node_one_new, node_two_new])
            old_first_terms = term_zero
            initial = jnp.where(is_head, start[0], received)
    return result[None]


def solution(mesh):
    placed = (
        P("tm", None, "space", None, None),
        P("space", None, None),
        P("space", None, None),
        P("space", None, None),
    )
    return jax.shard_map(
        per_device,
        mesh=mesh,
        in_specs=placed,
        out_specs=P("tm", None, "space", None, None),
        check_vma=False,
    )
```

profile of v0, /device:TPU:28, one launch (start us, length us, event | category | flops | bytes accessed | tf_op | source)
XLA Modules:
  0.0 97.2 jit_solution(13621230096489648600)
XLA Ops:
  0.0 1.1 %slice_bitcast_fusion.5 = f32[1,8,64,128]{3,2,1,0:T(8,128)S(1)} fusion(f32[1,2,8,64,128]{4,3,2,1,0:T(8,128)} %param.4), kind=kLoop, calls=%fused_computation.235 | loop fusion | bytes 524288 | tf_op jit(solution)/shard_map/squeeze | solution.py:89
  1.1 2.4 %collective-permute-start = (f32[1,1,64,128]{3,2,1,0:T(8,128)S(1)}, f32[1,1,64,128]{3,2,1,0:T(8,128)S(1)}, u32[]{:S(2)}, u32[]{:S(2)}) collective-permute-start(f32[1,1,64,128]{3,2,1,0:T(8,128)S(1)} %get-tuple-element.32), channel_id=1, source_target_pairs={{1,0},{2,1},{3,2},{5,4},{6,5},{7,6},{9,8},{10,9},{11,10},{13,12},{... | collective-permute-start | bytes 98312 | tf_op jit(solution)/shard_map/ppermute | solution.py:26
  3.5 1.3 %collective-permute-start.1 = (f32[1,1,64,128]{3,2,1,0:T(8,128)S(1)}, f32[1,1,64,128]{3,2,1,0:T(8,128)S(1)}, u32[]{:S(2)}, u32[]{:S(2)}) collective-permute-start(f32[1,1,64,128]{3,2,1,0:T(8,128)S(1)} %get-tuple-element.31), channel_id=1, source_target_pairs={{0,1},{1,2},{2,3},{4,5},{5,6},{6,7},{8,9},{9,10},{10,11},{12,13},{... | collective-permute-start | bytes 98312 | tf_op jit(solution)/shard_map/ppermute | solution.py:24
  4.8 1.2 %fusion.80 = f32[8,64,128]{2,1,0:T(8,128)S(1)} fusion(f32[8,64,128]{2,1,0:T(8,128)} %param.7, f32[1,2,8,64,128]{4,3,2,1,0:T(8,128)} %param.4), kind=kLoop, calls=%fused_computation.214 | loop fusion | flops 196608 | bytes 1048576 | tf_op jit(solution)/shard_map/mul | solution.py:62
  6.2 0.4 reduce_sum.117
  6.9 2.3 %collective-permute-done.1 = f32[1,1,64,128]{3,2,1,0:T(8,128)S(1)} collective-permute-done((f32[1,1,64,128]{3,2,1,0:T(8,128)S(1)}, f32[1,1,64,128]{3,2,1,0:T(8,128)S(1)}, u32[]{:S(2)}, u32[]{:S(2)}) %collective-permute-start.1) | collective-permute-done | bytes 32800 | tf_op jit(solution)/shard_map/ppermute | solution.py:24
  9.3 0.3 select_maximum_fusion.12
  9.5 0.4 fusion.63
  10.2 2.4 %collective-permute-start.2 = (f32[1,1,64,128]{3,2,1,0:T(8,128)S(1)}, f32[1,1,64,128]{3,2,1,0:T(8,128)S(1)}, u32[]{:S(2)}, u32[]{:S(2)}) collective-permute-start(f32[1,1,64,128]{3,2,1,0:T(8,128)S(1)} %get-tuple-element.30), channel_id=1, source_target_pairs={{1,0},{2,1},{3,2},{5,4},{6,5},{7,6},{9,8},{10,9},{11,10},{13,12},{... | collective-permute-start | bytes 98312 | tf_op jit(solution)/shard_map/ppermute | solution.py:26
  12.5 1.3 %collective-permute-start.3 = (f32[1,1,64,128]{3,2,1,0:T(8,128)S(1)}, f32[1,1,64,128]{3,2,1,0:T(8,128)S(1)}, u32[]{:S(2)}, u32[]{:S(2)}) collective-permute-start(f32[1,1,64,128]{3,2,1,0:T(8,128)S(1)} %get-tuple-element.29), channel_id=1, source_target_pairs={{0,1},{1,2},{2,3},{4,5},{5,6},{6,7},{8,9},{9,10},{10,11},{12,13},{... | collective-permute-start | bytes 98312 | tf_op jit(solution)/shard_map/ppermute | solution.py:24
  14.1 4.2 %collective-permute-done.3 = f32[1,1,64,128]{3,2,1,0:T(8,128)S(1)} collective-permute-done((f32[1,1,64,128]{3,2,1,0:T(8,128)S(1)}, f32[1,1,64,128]{3,2,1,0:T(8,128)S(1)}, u32[]{:S(2)}, u32[]{:S(2)}) %collective-permute-start.3) | collective-permute-done | bytes 32800 | tf_op jit(solution)/shard_map/ppermute | solution.py:24
  18.3 0.3 select_maximum_fusion.10
  18.6 0.3 fusion.58
  19.0 0.3 fusion.29
  19.3 2.4 %collective-permute-start.4 = (f32[1,1,64,128]{3,2,1,0:T(8,128)S(1)}, f32[1,1,64,128]{3,2,1,0:T(8,128)S(1)}, u32[]{:S(2)}, u32[]{:S(2)}) collective-permute-start(f32[1,1,64,128]{3,2,1,0:T(8,128)S(1)} %get-tuple-element.28), channel_id=1, source_target_pairs={{1,0},{2,1},{3,2},{5,4},{6,5},{7,6},{9,8},{10,9},{11,10},{13,12},{... | collective-permute-start | bytes 98312 | tf_op jit(solution)/shard_map/ppermute | solution.py:26
  21.7 1.3 %collective-permute-start.5 = (f32[1,1,64,128]{3,2,1,0:T(8,128)S(1)}, f32[1,1,64,128]{3,2,1,0:T(8,128)S(1)}, u32[]{:S(2)}, u32[]{:S(2)}) collective-permute-start(f32[1,1,64,128]{3,2,1,0:T(8,128)S(1)} %get-tuple-element.27), channel_id=1, source_target_pairs={{0,1},{1,2},{2,3},{4,5},{5,6},{6,7},{8,9},{9,10},{10,11},{12,13},{... | collective-permute-start | bytes 98312 | tf_op jit(solution)/shard_map/ppermute | solution.py:24
  23.3 4.2 %collective-permute-done.5 = f32[1,1,64,128]{3,2,1,0:T(8,128)S(1)} collective-permute-done((f32[1,1,64,128]{3,2,1,0:T(8,128)S(1)}, f32[1,1,64,128]{3,2,1,0:T(8,128)S(1)}, u32[]{:S(2)}, u32[]{:S(2)}) %collective-permute-start.5) | collective-permute-done | bytes 32800 | tf_op jit(solution)/shard_map/ppermute | solution.py:24
  27.5 0.3 select_maximum_fusion.8
  27.8 0.3 fusion.53
  28.2 0.4 add_reduce_fusion.3
  28.7 2.2 %collective-permute-start.6 = (f32[2,1,32,128]{3,2,1,0:T(8,128)S(1)}, f32[2,1,32,128]{3,2,1,0:T(8,128)S(1)}, u32[]{:S(2)}, u32[]{:S(2)}) collective-permute-start(f32[2,1,32,128]{3,2,1,0:T(8,128)S(1)} %get-tuple-element.36), channel_id=1, source_target_pairs={{1,0},{2,1},{3,2},{5,4},{6,5},{7,6},{9,8},{10,9},{11,10},{13,12},{... | collective-permute-start | bytes 98312 | tf_op jit(solution)/shard_map/ppermute | solution.py:26
  31.0 1.3 %collective-permute-start.7 = (f32[2,1,32,128]{3,2,1,0:T(8,128)S(1)}, f32[2,1,32,128]{3,2,1,0:T(8,128)S(1)}, u32[]{:S(2)}, u32[]{:S(2)}) collective-permute-start(f32[2,1,32,128]{3,2,1,0:T(8,128)S(1)} %get-tuple-element.35), channel_id=1, source_target_pairs={{0,1},{1,2},{2,3},{4,5},{5,6},{6,7},{8,9},{9,10},{10,11},{12,13},{... | collective-permute-start | bytes 98312 | tf_op jit(solution)/shard_map/ppermute | solution.py:24
  32.5 4.2 %collective-permute-done.7 = f32[2,1,32,128]{3,2,1,0:T(8,128)S(1)} collective-permute-done((f32[2,1,32,128]{3,2,1,0:T(8,128)S(1)}, f32[2,1,32,128]{3,2,1,0:T(8,128)S(1)}, u32[]{:S(2)}, u32[]{:S(2)}) %collective-permute-start.7) | collective-permute-done | bytes 32800 | tf_op jit(solution)/shard_map/ppermute | solution.py:24
  37.5 0.3 fusion.141
  38.2 1.0 %fusion.127 = (f32[2,8,64,128]{3,2,1,0:T(8,128)S(1)}, f32[2,1,8,64,128]{4,3,2,1,0:T(8,128)}) fusion(f32[1,2,8,64,128]{4,3,2,1,0:T(8,128)S(1)} %fusion.141, f32[1,2,8,64,128]{4,3,2,1,0:T(8,128)S(1)} %fusion.140, f32[8,64,128]{2,1,0:T(8,128)S(1)} %copy-done.1), kind=kLoop, calls=%fused_computation.301 | loop fusion | flops 786432 | bytes 2359296 | tf_op jit(solution)/shard_map/squeeze | solution.py:108
  39.2 0.7 fusion.131
  39.8 1.9 %collective-permute-start.11 = (f32[2,1,64,128]{3,2,1,0:T(8,128)}, f32[2,1,64,128]{3,2,1,0:T(8,128)S(1)}, u32[]{:S(2)}, u32[]{:S(2)}) collective-permute-start(f32[2,1,64,128]{3,2,1,0:T(8,128)} %get-tuple-element.14), channel_id=1, source_target_pairs={{1,0},{2,1},{3,2},{5,4},{6,5},{7,6},{9,8},{10,9},{11,10},{13,12},{... | collective-permute-start | bytes 196616 | tf_op jit(solution)/shard_map/ppermute | solution.py:26
  41.7 1.3 %collective-permute-start.12 = (f32[2,1,64,128]{3,2,1,0:T(8,128)}, f32[2,1,64,128]{3,2,1,0:T(8,128)S(1)}, u32[]{:S(2)}, u32[]{:S(2)}) collective-permute-start(f32[2,1,64,128]{3,2,1,0:T(8,128)} %get-tuple-element.13), channel_id=1, source_target_pairs={{0,1},{1,2},{2,3},{4,5},{5,6},{6,7},{8,9},{9,10},{10,11},{12,13},{... | collective-permute-start | bytes 196616 | tf_op jit(solution)/shard_map/ppermute | solution.py:24
  43.0 1.1 %fusion.24 = f32[2,8,64,128]{3,2,1,0:T(8,128)} fusion(f32[2,8,64,128]{3,2,1,0:T(8,128)S(1)} %bitcast.365, f32[1,2,8,64,128]{4,3,2,1,0:T(8,128)S(1)} %copy-done, f32[1,1,8,64,128]{4,3,2,1,0:T(8,128)S(1)} %bitcast.359, f32[1,1,8,64,128]{4,3,2,1,0:T(8,128)S(1)} %bitcast.363, f32[1,1,8,64,128]{4,3,2,1,0:T(8,128)S(1)} %bitcast.330, ...), kind=kLoop, calls=%fused_computation.72 | loop fusion | flops 2359296 | bytes 2621440 | tf_op jit(solution)/shard_map/add | solution.py:135
  44.1 1.9 %collective-permute-start.8 = (f32[2,8,64,128]{3,2,1,0:T(8,128)}, f32[2,8,64,128]{3,2,1,0:T(8,128)}, u32[]{:S(2)}, u32[]{:S(2)}) collective-permute-start(f32[2,8,64,128]{3,2,1,0:T(8,128)} %fusion.24), channel_id=1, source_target_pairs={{0,4},{4,8},{8,12},{12,16},{16,20},{20,24},{24,28},{1,5},{5,9},{9,... | collective-permute-start | bytes 1572872 | tf_op jit(solution)/shard_map/ppermute | solution.py:36
  46.1 2.0 %collective-permute-done.12 = f32[2,1,64,128]{3,2,1,0:T(8,128)S(1)} collective-permute-done((f32[2,1,64,128]{3,2,1,0:T(8,128)}, f32[2,1,64,128]{3,2,1,0:T(8,128)S(1)}, u32[]{:S(2)}, u32[]{:S(2)}) %collective-permute-start.12) | collective-permute-done | bytes 65568 | tf_op jit(solution)/shard_map/ppermute | solution.py:24
  48.1 0.4 select_maximum_fusion
  48.6 0.6 fusion.12
  49.2 6.6 %collective-permute-done.8 = f32[2,8,64,128]{3,2,1,0:T(8,128)} collective-permute-done((f32[2,8,64,128]{3,2,1,0:T(8,128)}, f32[2,8,64,128]{3,2,1,0:T(8,128)}, u32[]{:S(2)}, u32[]{:S(2)}) %collective-permute-start.8) | collective-permute-done | bytes 524320 | tf_op jit(solution)/shard_map/ppermute | solution.py:36
  55.8 1.1 %bitcast_select_fusion = f32[2,8,64,128]{3,2,1,0:T(8,128)S(1)} fusion(f32[2,8,64,128]{3,2,1,0:T(8,128)} %collective-permute-done.8, f32[1,2,8,64,128]{4,3,2,1,0:T(8,128)S(1)} %copy-done, pred[]{:T(512)S(6)} %eq.3), kind=kLoop, calls=%fused_computation.84 | loop fusion | flops 131072 | bytes 1572865 | tf_op jit(solution)/shard_map/jit(_where)/select_n | solution.py:143
  57.0 4.5 %collective-permute-start.9 = (f32[1,1,64,128]{3,2,1,0:T(8,128)S(1)}, f32[1,1,64,128]{3,2,1,0:T(8,128)S(1)}, u32[]{:S(2)}, u32[]{:S(2)}) collective-permute-start(f32[1,1,64,128]{3,2,1,0:T(8,128)S(1)} %get-tuple-element.24), channel_id=1, source_target_pairs={{1,0},{2,1},{3,2},{5,4},{6,5},{7,6},{9,8},{10,9},{11,10},{13,12},{... | collective-permute-start | bytes 98312 | tf_op jit(solution)/shard_map/ppermute | solution.py:26
  61.5 1.3 %collective-permute-start.10 = (f32[1,1,64,128]{3,2,1,0:T(8,128)S(1)}, f32[1,1,64,128]{3,2,1,0:T(8,128)S(1)}, u32[]{:S(2)}, u32[]{:S(2)}) collective-permute-start(f32[1,1,64,128]{3,2,1,0:T(8,128)S(1)} %get-tuple-element.23), channel_id=1, source_target_pairs={{0,1},{1,2},{2,3},{4,5},{5,6},{6,7},{8,9},{9,10},{10,11},{12,13},{... | collective-permute-start | bytes 98312 | tf_op jit(solution)/shard_map/ppermute | solution.py:24
  62.9 0.4 reduce_sum.125
  63.3 4.1 %collective-permute-done.10 = f32[1,1,64,128]{3,2,1,0:T(8,128)S(1)} collective-permute-done((f32[1,1,64,128]{3,2,1,0:T(8,128)S(1)}, f32[1,1,64,128]{3,2,1,0:T(8,128)S(1)}, u32[]{:S(2)}, u32[]{:S(2)}) %collective-permute-start.10) | collective-permute-done | bytes 32800 | tf_op jit(solution)/shard_map/ppermute | solution.py:24
  67.3 0.3 select_maximum_fusion.6
  67.6 0.4 fusion.48
  68.0 0.7 copy-done.6
  68.6 0.3 fusion.18
  69.0 1.9 %collective-permute-start.13 = (f32[1,1,64,128]{3,2,1,0:T(8,128)S(1)}, f32[1,1,64,128]{3,2,1,0:T(8,128)S(1)}, u32[]{:S(2)}, u32[]{:S(2)}) collective-permute-start(f32[1,1,64,128]{3,2,1,0:T(8,128)S(1)} %get-tuple-element.20), channel_id=1, source_target_pairs={{1,0},{2,1},{3,2},{5,4},{6,5},{7,6},{9,8},{10,9},{11,10},{13,12},{... | collective-permute-start | bytes 98312 | tf_op jit(solution)/shard_map/ppermute | solution.py:26
  71.0 1.3 %collective-permute-start.14 = (f32[1,1,64,128]{3,2,1,0:T(8,128)S(1)}, f32[1,1,64,128]{3,2,1,0:T(8,128)S(1)}, u32[]{:S(2)}, u32[]{:S(2)}) collective-permute-start(f32[1,1,64,128]{3,2,1,0:T(8,128)S(1)} %get-tuple-element.19), channel_id=1, source_target_pairs={{0,1},{1,2},{2,3},{4,5},{5,6},{6,7},{8,9},{9,10},{10,11},{12,13},{... | collective-permute-start | bytes 98312 | tf_op jit(solution)/shard_map/ppermute | solution.py:24
  72.3 0.7 copy_dynamic-update-slice_fusion.3
  73.0 0.4 reduce_sum.127
  73.4 0.7 copy_dynamic-update-slice_fusion.2
  74.2 2.6 %collective-permute-done.14 = f32[1,1,64,128]{3,2,1,0:T(8,128)S(1)} collective-permute-done((f32[1,1,64,128]{3,2,1,0:T(8,128)S(1)}, f32[1,1,64,128]{3,2,1,0:T(8,128)S(1)}, u32[]{:S(2)}, u32[]{:S(2)}) %collective-permute-start.14) | collective-permute-done | bytes 32800 | tf_op jit(solution)/shard_map/ppermute | solution.py:24
  76.8 0.3 select_maximum_fusion.4
  77.1 0.4 fusion.43
  77.4 0.7 copy-done.7
  78.1 0.3 fusion.22
  78.5 2.0 %collective-permute-start.15 = (f32[1,1,64,128]{3,2,1,0:T(8,128)S(1)}, f32[1,1,64,128]{3,2,1,0:T(8,128)S(1)}, u32[]{:S(2)}, u32[]{:S(2)}) collective-permute-start(f32[1,1,64,128]{3,2,1,0:T(8,128)S(1)} %get-tuple-element.18), channel_id=1, source_target_pairs={{1,0},{2,1},{3,2},{5,4},{6,5},{7,6},{9,8},{10,9},{11,10},{13,12},{... | collective-permute-start | bytes 98312 | tf_op jit(solution)/shard_map/ppermute | solution.py:26
  80.4 1.3 %collective-permute-start.16 = (f32[1,1,64,128]{3,2,1,0:T(8,128)S(1)}, f32[1,1,64,128]{3,2,1,0:T(8,128)S(1)}, u32[]{:S(2)}, u32[]{:S(2)}) collective-permute-start(f32[1,1,64,128]{3,2,1,0:T(8,128)S(1)} %get-tuple-element.17), channel_id=1, source_target_pairs={{0,1},{1,2},{2,3},{4,5},{5,6},{6,7},{8,9},{9,10},{10,11},{12,13},{... | collective-permute-start | bytes 98312 | tf_op jit(solution)/shard_map/ppermute | solution.py:24
  82.0 4.2 %collective-permute-done.16 = f32[1,1,64,128]{3,2,1,0:T(8,128)S(1)} collective-permute-done((f32[1,1,64,128]{3,2,1,0:T(8,128)S(1)}, f32[1,1,64,128]{3,2,1,0:T(8,128)S(1)}, u32[]{:S(2)}, u32[]{:S(2)}) %collective-permute-start.16) | collective-permute-done | bytes 32800 | tf_op jit(solution)/shard_map/ppermute | solution.py:24
  86.2 0.3 select_maximum_fusion.2
  86.5 0.4 fusion.38
  86.9 0.6 copy-done.12
  87.9 1.9 %collective-permute-start.17 = (f32[2,1,32,128]{3,2,1,0:T(8,128)S(1)}, f32[2,1,32,128]{3,2,1,0:T(8,128)S(1)}, u32[]{:S(2)}, u32[]{:S(2)}) collective-permute-start(f32[2,1,32,128]{3,2,1,0:T(8,128)S(1)} %get-tuple-element.34), channel_id=1, source_target_pairs={{1,0},{2,1},{3,2},{5,4},{6,5},{7,6},{9,8},{10,9},{11,10},{13,12},{... | collective-permute-start | bytes 98312 | tf_op jit(solution)/shard_map/ppermute | solution.py:26
  89.8 1.3 %collective-permute-start.18 = (f32[2,1,32,128]{3,2,1,0:T(8,128)S(1)}, f32[2,1,32,128]{3,2,1,0:T(8,128)S(1)}, u32[]{:S(2)}, u32[]{:S(2)}) collective-permute-start(f32[2,1,32,128]{3,2,1,0:T(8,128)S(1)} %get-tuple-element.33), channel_id=1, source_target_pairs={{0,1},{1,2},{2,3},{4,5},{5,6},{6,7},{8,9},{9,10},{10,11},{12,13},{... | collective-permute-start | bytes 98312 | tf_op jit(solution)/shard_map/ppermute | solution.py:24
  91.1 0.4 reduce_sum.129
  91.5 4.1 %collective-permute-done.18 = f32[2,1,32,128]{3,2,1,0:T(8,128)S(1)} collective-permute-done((f32[2,1,32,128]{3,2,1,0:T(8,128)S(1)}, f32[2,1,32,128]{3,2,1,0:T(8,128)S(1)}, u32[]{:S(2)}, u32[]{:S(2)}) %collective-permute-start.18) | collective-permute-done | bytes 32800 | tf_op jit(solution)/shard_map/ppermute | solution.py:24
  96.3 0.9 add_bitcast_fusion
  (94 shorter events, 4.4 us)
Async XLA Ops:
  0.0 6.2 %copy-start = (f32[1,2,8,64,128]{4,3,2,1,0:T(8,128)S(1)}, f32[1,2,8,64,128]{4,3,2,1,0:T(8,128)}, u32[]{:S(2)}) copy-start(f32[1,2,8,64,128]{4,3,2,1,0:T(8,128)} %param.4) | copy-start | bytes 1572868
  0.0 5.9 %copy-start.1 = (f32[8,64,128]{2,1,0:T(8,128)S(1)}, f32[8,64,128]{2,1,0:T(8,128)}, u32[]{:S(2)}) copy-start(f32[8,64,128]{2,1,0:T(8,128)} %param.7) | copy-start | bytes 786436
  0.0 6.5 %copy-start.2 = (f32[8,64,128]{2,1,0:T(8,128)S(1)}, f32[8,64,128]{2,1,0:T(8,128)}, u32[]{:S(2)}) copy-start(f32[8,64,128]{2,1,0:T(8,128)} %param.6) | copy-start | bytes 786436
  0.0 6.7 %copy-start.3 = (f32[8,64,128]{2,1,0:T(8,128)S(1)}, f32[8,64,128]{2,1,0:T(8,128)}, u32[]{:S(2)}) copy-start(f32[8,64,128]{2,1,0:T(8,128)} %param.5) | copy-start | bytes 786436
  1.1 5.8 %collective-permute-start = (f32[1,1,64,128]{3,2,1,0:T(8,128)S(1)}, f32[1,1,64,128]{3,2,1,0:T(8,128)S(1)}, u32[]{:S(2)}, u32[]{:S(2)}) collective-permute-start(f32[1,1,64,128]{3,2,1,0:T(8,128)S(1)} %get-tuple-element.32), channel_id=1, source_target_pairs={{1,0},{2,1},{3,2},{5,4},{6,5},{7,6},{9,8},{10,9},{11,10},{13,12},{... | collective-permute-start | bytes 98312 | tf_op jit(solution)/shard_map/ppermute | solution.py:26
  3.5 5.8 %collective-permute-start.1 = (f32[1,1,64,128]{3,2,1,0:T(8,128)S(1)}, f32[1,1,64,128]{3,2,1,0:T(8,128)S(1)}, u32[]{:S(2)}, u32[]{:S(2)}) collective-permute-start(f32[1,1,64,128]{3,2,1,0:T(8,128)S(1)} %get-tuple-element.31), channel_id=1, source_target_pairs={{0,1},{1,2},{2,3},{4,5},{5,6},{6,7},{8,9},{9,10},{10,11},{12,13},{... | collective-permute-start | bytes 98312 | tf_op jit(solution)/shard_map/ppermute | solution.py:24
  6.1 22.5 %copy-start.13 = (f32[4,32,128]{2,1,0:T(8,128)}, f32[4,32,128]{2,1,0:T(8,128)S(1)}, u32[]{:S(2)}) copy-start(f32[4,32,128]{2,1,0:T(8,128)S(1)} %broadcast_multiply_fusion) | copy-start | bytes 196612
  10.2 3.9 %collective-permute-start.2 = (f32[1,1,64,128]{3,2,1,0:T(8,128)S(1)}, f32[1,1,64,128]{3,2,1,0:T(8,128)S(1)}, u32[]{:S(2)}, u32[]{:S(2)}) collective-permute-start(f32[1,1,64,128]{3,2,1,0:T(8,128)S(1)} %get-tuple-element.30), channel_id=1, source_target_pairs={{1,0},{2,1},{3,2},{5,4},{6,5},{7,6},{9,8},{10,9},{11,10},{13,12},{... | collective-permute-start | bytes 98312 | tf_op jit(solution)/shard_map/ppermute | solution.py:26
  12.5 5.8 %collective-permute-start.3 = (f32[1,1,64,128]{3,2,1,0:T(8,128)S(1)}, f32[1,1,64,128]{3,2,1,0:T(8,128)S(1)}, u32[]{:S(2)}, u32[]{:S(2)}) collective-permute-start(f32[1,1,64,128]{3,2,1,0:T(8,128)S(1)} %get-tuple-element.29), channel_id=1, source_target_pairs={{0,1},{1,2},{2,3},{4,5},{5,6},{6,7},{8,9},{9,10},{10,11},{12,13},{... | collective-permute-start | bytes 98312 | tf_op jit(solution)/shard_map/ppermute | solution.py:24
  19.3 3.9 %collective-permute-start.4 = (f32[1,1,64,128]{3,2,1,0:T(8,128)S(1)}, f32[1,1,64,128]{3,2,1,0:T(8,128)S(1)}, u32[]{:S(2)}, u32[]{:S(2)}) collective-permute-start(f32[1,1,64,128]{3,2,1,0:T(8,128)S(1)} %get-tuple-element.28), channel_id=1, source_target_pairs={{1,0},{2,1},{3,2},{5,4},{6,5},{7,6},{9,8},{10,9},{11,10},{13,12},{... | collective-permute-start | bytes 98312 | tf_op jit(solution)/shard_map/ppermute | solution.py:26
  21.7 5.8 %collective-permute-start.5 = (f32[1,1,64,128]{3,2,1,0:T(8,128)S(1)}, f32[1,1,64,128]{3,2,1,0:T(8,128)S(1)}, u32[]{:S(2)}, u32[]{:S(2)}) collective-permute-start(f32[1,1,64,128]{3,2,1,0:T(8,128)S(1)} %get-tuple-element.27), channel_id=1, source_target_pairs={{0,1},{1,2},{2,3},{4,5},{5,6},{6,7},{8,9},{9,10},{10,11},{12,13},{... | collective-permute-start | bytes 98312 | tf_op jit(solution)/shard_map/ppermute | solution.py:24
  28.7 3.8 %collective-permute-start.6 = (f32[2,1,32,128]{3,2,1,0:T(8,128)S(1)}, f32[2,1,32,128]{3,2,1,0:T(8,128)S(1)}, u32[]{:S(2)}, u32[]{:S(2)}) collective-permute-start(f32[2,1,32,128]{3,2,1,0:T(8,128)S(1)} %get-tuple-element.36), channel_id=1, source_target_pairs={{1,0},{2,1},{3,2},{5,4},{6,5},{7,6},{9,8},{10,9},{11,10},{13,12},{... | collective-permute-start | bytes 98312 | tf_op jit(solution)/shard_map/ppermute | solution.py:26
  31.0 5.8 %collective-permute-start.7 = (f32[2,1,32,128]{3,2,1,0:T(8,128)S(1)}, f32[2,1,32,128]{3,2,1,0:T(8,128)S(1)}, u32[]{:S(2)}, u32[]{:S(2)}) collective-permute-start(f32[2,1,32,128]{3,2,1,0:T(8,128)S(1)} %get-tuple-element.35), channel_id=1, source_target_pairs={{0,1},{1,2},{2,3},{4,5},{5,6},{6,7},{8,9},{9,10},{10,11},{12,13},{... | collective-permute-start | bytes 98312 | tf_op jit(solution)/shard_map/ppermute | solution.py:24
  32.3 5.0 %copy-start.15 = (f32[4,32,128]{2,1,0:T(8,128)}, f32[4,32,128]{2,1,0:T(8,128)S(1)}, u32[]{:S(2)}) copy-start(f32[4,32,128]{2,1,0:T(8,128)S(1)} %get-tuple-element.39) | copy-start | bytes 196612
  32.3 5.0 %copy-start.17 = (f32[4,32,128]{2,1,0:T(8,128)}, f32[4,32,128]{2,1,0:T(8,128)S(1)}, u32[]{:S(2)}) copy-start(f32[4,32,128]{2,1,0:T(8,128)S(1)} %get-tuple-element.40) | copy-start | bytes 196612
  38.2 5.9 %copy-start.4 = (f32[1,2,8,64,128]{4,3,2,1,0:T(8,128)}, f32[1,2,8,64,128]{4,3,2,1,0:T(8,128)S(1)}, u32[]{:S(2)}) copy-start(f32[1,2,8,64,128]{4,3,2,1,0:T(8,128)S(1)} %fusion.140) | copy-start | bytes 1572868
  39.8 6.2 %collective-permute-start.11 = (f32[2,1,64,128]{3,2,1,0:T(8,128)}, f32[2,1,64,128]{3,2,1,0:T(8,128)S(1)}, u32[]{:S(2)}, u32[]{:S(2)}) collective-permute-start(f32[2,1,64,128]{3,2,1,0:T(8,128)} %get-tuple-element.14), channel_id=1, source_target_pairs={{1,0},{2,1},{3,2},{5,4},{6,5},{7,6},{9,8},{10,9},{11,10},{13,12},{... | collective-permute-start | bytes 196616 | tf_op jit(solution)/shard_map/ppermute | solution.py:26
  41.7 6.4 %collective-permute-start.12 = (f32[2,1,64,128]{3,2,1,0:T(8,128)}, f32[2,1,64,128]{3,2,1,0:T(8,128)S(1)}, u32[]{:S(2)}, u32[]{:S(2)}) collective-permute-start(f32[2,1,64,128]{3,2,1,0:T(8,128)} %get-tuple-element.13), channel_id=1, source_target_pairs={{0,1},{1,2},{2,3},{4,5},{5,6},{6,7},{8,9},{9,10},{10,11},{12,13},{... | collective-permute-start | bytes 196616 | tf_op jit(solution)/shard_map/ppermute | solution.py:24
  44.1 11.7 %collective-permute-start.8 = (f32[2,8,64,128]{3,2,1,0:T(8,128)}, f32[2,8,64,128]{3,2,1,0:T(8,128)}, u32[]{:S(2)}, u32[]{:S(2)}) collective-permute-start(f32[2,8,64,128]{3,2,1,0:T(8,128)} %fusion.24), channel_id=1, source_target_pairs={{0,4},{4,8},{8,12},{12,16},{16,20},{20,24},{24,28},{1,5},{5,9},{9,... | collective-permute-start | bytes 1572872 | tf_op jit(solution)/shard_map/ppermute | solution.py:36
  46.1 2.5 %copy-start.5 = (f32[1,2,8,64,128]{4,3,2,1,0:T(8,128)S(1)}, f32[1,2,8,64,128]{4,3,2,1,0:T(8,128)}, u32[]{:S(2)}) copy-start(f32[1,2,8,64,128]{4,3,2,1,0:T(8,128)} %copy-done.4) | copy-start | bytes 1572868
  57.0 6.3 %collective-permute-start.9 = (f32[1,1,64,128]{3,2,1,0:T(8,128)S(1)}, f32[1,1,64,128]{3,2,1,0:T(8,128)S(1)}, u32[]{:S(2)}, u32[]{:S(2)}) collective-permute-start(f32[1,1,64,128]{3,2,1,0:T(8,128)S(1)} %get-tuple-element.24), channel_id=1, source_target_pairs={{1,0},{2,1},{3,2},{5,4},{6,5},{7,6},{9,8},{10,9},{11,10},{13,12},{... | collective-permute-start | bytes 98312 | tf_op jit(solution)/shard_map/ppermute | solution.py:26
  61.5 5.8 %collective-permute-start.10 = (f32[1,1,64,128]{3,2,1,0:T(8,128)S(1)}, f32[1,1,64,128]{3,2,1,0:T(8,128)S(1)}, u32[]{:S(2)}, u32[]{:S(2)}) collective-permute-start(f32[1,1,64,128]{3,2,1,0:T(8,128)S(1)} %get-tuple-element.23), channel_id=1, source_target_pairs={{0,1},{1,2},{2,3},{4,5},{5,6},{6,7},{8,9},{9,10},{10,11},{12,13},{... | collective-permute-start | bytes 98312 | tf_op jit(solution)/shard_map/ppermute | solution.py:24
  62.9 5.1 %copy-start.10 = (f32[8,64,128]{2,1,0:T(8,128)}, f32[8,64,128]{2,1,0:T(8,128)S(1)}, u32[]{:S(2)}) copy-start(f32[8,64,128]{2,1,0:T(8,128)S(1)} %fusion.71) | copy-start | bytes 786436
  67.6 1.0 %copy-start.6 = (f32[2,1,8,64,128]{4,3,2,1,0:T(8,128)S(1)}, f32[2,1,8,64,128]{4,3,2,1,0:T(8,128)}, u32[]{:S(2)}) copy-start(f32[2,1,8,64,128]{4,3,2,1,0:T(8,128)} %get-tuple-element.12) | copy-start | bytes 1572868
  68.9 4.4 %copy-start.11 = (f32[8,64,128]{2,1,0:T(8,128)S(1)}, f32[8,64,128]{2,1,0:T(8,128)}, u32[]{:S(2)}) copy-start(f32[8,64,128]{2,1,0:T(8,128)} %copy-done.10) | copy-start | bytes 786436
  69.0 5.2 %copy-start.8 = (f32[8,64,128]{2,1,0:T(8,128)}, f32[8,64,128]{2,1,0:T(8,128)S(1)}, u32[]{:S(2)}) copy-start(f32[8,64,128]{2,1,0:T(8,128)S(1)} %fusion.68) | copy-start | bytes 786436
  69.0 5.1 %collective-permute-start.13 = (f32[1,1,64,128]{3,2,1,0:T(8,128)S(1)}, f32[1,1,64,128]{3,2,1,0:T(8,128)S(1)}, u32[]{:S(2)}, u32[]{:S(2)}) collective-permute-start(f32[1,1,64,128]{3,2,1,0:T(8,128)S(1)} %get-tuple-element.20), channel_id=1, source_target_pairs={{1,0},{2,1},{3,2},{5,4},{6,5},{7,6},{9,8},{10,9},{11,10},{13,12},{... | collective-permute-start | bytes 98312 | tf_op jit(solution)/shard_map/ppermute | solution.py:26
  71.0 5.8 %collective-permute-start.14 = (f32[1,1,64,128]{3,2,1,0:T(8,128)S(1)}, f32[1,1,64,128]{3,2,1,0:T(8,128)S(1)}, u32[]{:S(2)}, u32[]{:S(2)}) collective-permute-start(f32[1,1,64,128]{3,2,1,0:T(8,128)S(1)} %get-tuple-element.19), channel_id=1, source_target_pairs={{0,1},{1,2},{2,3},{4,5},{5,6},{6,7},{8,9},{9,10},{10,11},{12,13},{... | collective-permute-start | bytes 98312 | tf_op jit(solution)/shard_map/ppermute | solution.py:24
  77.0 1.0 %copy-start.7 = (f32[2,1,8,64,128]{4,3,2,1,0:T(8,128)S(1)}, f32[2,1,8,64,128]{4,3,2,1,0:T(8,128)}, u32[]{:S(2)}) copy-start(f32[2,1,8,64,128]{4,3,2,1,0:T(8,128)} %get-tuple-element.12) | copy-start | bytes 1572868
  77.0 1.1 %copy-start.9 = (f32[8,64,128]{2,1,0:T(8,128)S(1)}, f32[8,64,128]{2,1,0:T(8,128)}, u32[]{:S(2)}) copy-start(f32[8,64,128]{2,1,0:T(8,128)} %copy-done.8) | copy-start | bytes 786436
  78.5 3.5 %collective-permute-start.15 = (f32[1,1,64,128]{3,2,1,0:T(8,128)S(1)}, f32[1,1,64,128]{3,2,1,0:T(8,128)S(1)}, u32[]{:S(2)}, u32[]{:S(2)}) collective-permute-start(f32[1,1,64,128]{3,2,1,0:T(8,128)S(1)} %get-tuple-element.18), channel_id=1, source_target_pairs={{1,0},{2,1},{3,2},{5,4},{6,5},{7,6},{9,8},{10,9},{11,10},{13,12},{... | collective-permute-start | bytes 98312 | tf_op jit(solution)/shard_map/ppermute | solution.py:26
  80.4 5.8 %collective-permute-start.16 = (f32[1,1,64,128]{3,2,1,0:T(8,128)S(1)}, f32[1,1,64,128]{3,2,1,0:T(8,128)S(1)}, u32[]{:S(2)}, u32[]{:S(2)}) collective-permute-start(f32[1,1,64,128]{3,2,1,0:T(8,128)S(1)} %get-tuple-element.17), channel_id=1, source_target_pairs={{0,1},{1,2},{2,3},{4,5},{5,6},{6,7},{8,9},{9,10},{10,11},{12,13},{... | collective-permute-start | bytes 98312 | tf_op jit(solution)/shard_map/ppermute | solution.py:24
  86.5 1.0 %copy-start.12 = (f32[2,4,2,32,2,128]{5,3,4,2,1,0:T(8,128)S(1)}, f32[2,4,2,32,2,128]{5,3,4,2,1,0:T(8,128)}, u32[]{:S(2)}) copy-start(f32[2,4,2,32,2,128]{5,3,4,2,1,0:T(8,128)} %copy_dynamic-update-slice_fusion.2) | copy-start | bytes 1572868
  86.9 0.9 copy-start.14
  87.7 8.1 %copy-start.16 = (f32[4,32,128]{2,1,0:T(8,128)S(1)}, f32[4,32,128]{2,1,0:T(8,128)}, u32[]{:S(2)}) copy-start(f32[4,32,128]{2,1,0:T(8,128)} %copy-done.15) | copy-start | bytes 196612
  87.8 8.1 %copy-start.18 = (f32[4,32,128]{2,1,0:T(8,128)S(1)}, f32[4,32,128]{2,1,0:T(8,128)}, u32[]{:S(2)}) copy-start(f32[4,32,128]{2,1,0:T(8,128)} %copy-done.17) | copy-start | bytes 196612
  87.9 3.6 %collective-permute-start.17 = (f32[2,1,32,128]{3,2,1,0:T(8,128)S(1)}, f32[2,1,32,128]{3,2,1,0:T(8,128)S(1)}, u32[]{:S(2)}, u32[]{:S(2)}) collective-permute-start(f32[2,1,32,128]{3,2,1,0:T(8,128)S(1)} %get-tuple-element.34), channel_id=1, source_target_pairs={{1,0},{2,1},{3,2},{5,4},{6,5},{7,6},{9,8},{10,9},{11,10},{13,12},{... | collective-permute-start | bytes 98312 | tf_op jit(solution)/shard_map/ppermute | solution.py:26
  89.8 5.8 %collective-permute-start.18 = (f32[2,1,32,128]{3,2,1,0:T(8,128)S(1)}, f32[2,1,32,128]{3,2,1,0:T(8,128)S(1)}, u32[]{:S(2)}, u32[]{:S(2)}) collective-permute-start(f32[2,1,32,128]{3,2,1,0:T(8,128)S(1)} %get-tuple-element.33), channel_id=1, source_target_pairs={{0,1},{1,2},{2,3},{4,5},{5,6},{6,7},{8,9},{9,10},{10,11},{12,13},{... | collective-permute-start | bytes 98312 | tf_op jit(solution)/shard_map/ppermute | solution.py:24
where the time goes:
time: 98 us; the launch traced here: 97.2 us
  waiting for transfers between devices  39.6 us (40%)
  starting transfers between devices  35.1 us (36%)
  other arithmetic  15.3 us (16%)
  local copies, waits for them, and re-layouts  6.22 us (6%)
    ppermute x9, waiting for transfers between devices, extended(): lax.ppermute(tail, axis, [(i, (i + 1) % count) for i in range(ends)])  32.1 us
    ppermute x9, starting transfers between devices, extended(): lax.ppermute(head, axis, [((i + 1) % count, i) for i in range(ends)])  21.6 us
    ppermute x9, starting transfers between devices, extended(): lax.ppermute(tail, axis, [(i, (i + 1) % count) for i in range(ends)])  11.6 us
    ppermute x1, waiting for transfers between devices, passed_along(): return lax.ppermute(array, axis, pairs)  6.63 us
    unnamed x43, local copies, waits for them, and re-layouts  2.89 us
    reduce_sum x9, other arithmetic, restrict(): return 0.25 * jnp.sum(blocks, axis=(-4, -2))  2.67 us
    concatenate x9, other arithmetic, extended(): jnp.concatenate([lax.ppermute(tail, axis, [(i, (i + 1) % count) for i in...  2.39 us
    sub x6, other arithmetic, forces(): conduct * laplace  2.1 us
  transfers between devices with their start and end apart: 19, of which 14 were waited for; matrix products, arithmetic and copies ran while one was open for 7% of the time, Pallas kernels for 0%

commit v1 on v0

v1 whole, which is shorter than its diff:
```python
import functools
import jax
import jax.numpy as jnp
from jax import lax
from jax.experimental import pallas as pl
from jax.experimental.pallas import tpu as pltpu
from jax.sharding import PartitionSpec as P

MESH = pl.DeviceIdType.MESH
SIXTH = 1.0 / 6.0
W24 = 1.0 / 24.0


def react(e, t):
    return 2.0 * e * (1.0 - e) * (e - t)


def near(v, axis, by):
    n = v.shape[axis]
    at = lax.broadcasted_iota(jnp.int32, v.shape, axis)
    low = jnp.where(at < by, 0.0, pltpu.roll(v, by, axis))
    high = jnp.where(at >= n - by, 0.0, pltpu.roll(v, n - by, axis))
    return low + high


def tiles(v, by):
    rows, lanes = v.shape
    return pltpu.roll(v.reshape(rows // 8, 8, lanes), by, 1).reshape(rows, lanes)


def even_rows(v):
    return lax.broadcasted_iota(jnp.int32, v.shape, 0) % 2 == 0


def pair(v):
    return v + jnp.where(even_rows(v), tiles(v, 7), tiles(v, 1))


def fold(v):
    half = v.shape[0] // 2
    return jnp.where(even_rows(v[:half]), v[:half], v[half:])


def expand(x):
    even = even_rows(x)
    return jnp.where(even, x, tiles(x, 1)), jnp.where(even, tiles(x, 7), x)


def unfold(x):
    return jnp.concatenate(expand(x), axis=0)


def inplane(e):
    return near(e, 0, 1) + near(e, 1, 1) - 6.0 * e


MESSAGES = {
    name: at
    for at, name in enumerate(
        [
            (kind, side)
            for kind in ("q", "c", "n1p", "n2", "dp", "n2x", "j", "jx", "m1", "m2p", "d2")
            for side in (0, 1)
        ]
        + ["n2r", "n2e", "jt"]
    )
}


def kernel(
    start, cond, thr, rec, out,
    qe, qr, c, t, k, cc, tc, kc,
    f0e, f0r, n1e, n1r, n2e, n2r, t1e, t1r,
    dE, dR, jE, jR, u1e, u2e, s1e, s1r, s2e, s2r,
    qne, qnr, m1e, m1r, m2e, m2r, t0e, t0r, oe, orr,
    n1s, n1h, ds, dh, js, jh, jxh, n2xh, rn2r, rn2e, jts, jth,
    m2s, m2h, d2s, d2h,
    load_sem, store_sem, send_sem, recv_sem,
):
    nx = qr.shape[0]
    cn = nx // 2
    p, s = lax.axis_index("tm"), lax.axis_index("space")
    slices, slabs = lax.axis_size("tm"), lax.axis_size("space")
    head = p == 0
    has = (s > 0, s < slabs - 1)
    earlier, later = p > 0, p < slices - 1
    plane = qe.shape[1:]
    zeros = jnp.zeros(plane, jnp.float32)

    loads = [
        pltpu.make_async_copy(src, dst, load_sem.at[i])
        for i, (src, dst) in enumerate(
            [
                (start.at[0, 0], qe.at[pl.ds(1, nx)]),
                (cond, c.at[pl.ds(1, nx)]),
                (thr, t),
                (start.at[0, 1], qr),
                (rec, k),
            ]
        )
    ]
    for load in loads:
        load.start()

    barrier = pltpu.get_barrier_semaphore()

    def greet(when, dp, dside):
        @pl.when(when)
        def _():
            pl.semaphore_signal(barrier, inc=1, device_id=(p + dp, s + dside), device_id_type=MESH)

    greet(has[0], 0, -1)
    greet(has[1], 0, 1)
    greet(earlier, -1, 0)
    greet(earlier & has[0], -1, -1)
    greet(earlier & has[1], -1, 1)

    for side in (0, 1):
        end = side * (nx + 1)

        @pl.when(jnp.logical_not(has[side]))
        def _():
            for ref in (qe, c):
                ref[end] = zeros
            for ref in (n1h, n2xh, m2h):
                ref[side] = zeros
            n2e[end] = zeros
            m1e[end] = zeros
            for ref in (dh, jh, jxh, d2h):
                ref[side] = zeros[: plane[0] // 2]

    sides = has[0].astype(jnp.int32) + has[1].astype(jnp.int32)
    after = later.astype(jnp.int32)
    pl.semaphore_wait(barrier, sides + after * (sides + 1))

    pending = []

    def copy_of(name, src, dst, dp, dside):
        at = MESSAGES[name]
        return pltpu.make_async_remote_copy(
            src_ref=src,
            dst_ref=dst,
            send_sem=send_sem.at[at],
            recv_sem=recv_sem.at[at],
            device_id=(p + dp, s + dside),
            device_id_type=MESH,
        )

    def send(name, src, dst, when, dp=0, dside=0):
        @pl.when(when)
        def _():
            copy_of(name, src, dst, dp, dside).start()

        pending.append((name, src, dst, when, dp, dside))

    def receive(name, dst, when):
        @pl.when(when)
        def _():
            copy_of(name, dst, dst, 0, 0).wait_recv()

    def to_sides(kind, src, dst):
        for side in (0, 1):
            send((kind, side), src(side), dst(1 - side), has[side], 0, 2 * side - 1)

    def to_later_sides(kind, src, dst):
        for side in (0, 1):
            send((kind, side), src(side), dst(1 - side), later & has[side], 1, 2 * side - 1)

    def from_side(kind, side, dst, when=None):
        receive((kind, 1 - side), dst, has[side] if when is None else when & has[side])

    def edge(side):
        return side * (nx - 1)

    def halo(ref):
        return lambda side: ref.at[side * (ref.shape[0] - 1)]

    def slot(ref):
        return lambda side: ref.at[side]

    def each(low, high, body):
        def step(i, _):
            body(i)
            return 0

        lax.fori_loop(low, high, step, 0)

    def on_edges(body):
        each(0, 2, lambda side: body(side, side * (nx - 1), 2 + side * (nx - 3)))

    to_sides("q", lambda side: start.at[0, 0, edge(side)], halo(qe))
    to_sides("c", lambda side: cond.at[edge(side)], halo(c))
    for load in loads:
        load.wait()

    def first_edge(side, i, inner):
        e, r = qe[i + 1], qr[i]
        f = c[i + 1] * (qe[inner] + inplane(e)) + react(e, t[i]) - r
        g = k[i] * (e - 0.5 * r)
        f0e[i], f0r[i] = f, g
        n1 = e + 0.5 * f
        n1e[i + 1], n1s[side], n1r[i] = n1, n1, r + 0.5 * g

    on_edges(first_edge)
    to_sides("n1p", slot(n1s), slot(n1h))

    def slow_step(i):
        g = k[i] * (n1e[i + 1] - 0.5 * n1r[i])
        t1r[i] = g
        n2r[i] = n1r[i] + 0.5 * g

    def first_inner(i):
        e, r = qe[i + 1], qr[i]
        f = c[i + 1] * (qe[i] + qe[i + 2] + inplane(e)) + react(e, t[i]) - r
        g = k[i] * (e - 0.5 * r)
        f0e[i], f0r[i] = f, g
        n1e[i + 1], n1r[i] = e + 0.5 * f, r + 0.5 * g
        slow_step(i)

    each(1, nx - 1, first_inner)

    def coarse_coeffs(j):
        for fine, shift, coarse in ((c, 1, cc), (t, 0, tc), (k, 0, kc)):
            coarse[j] = 0.25 * pair(fine[2 * j + shift] + fine[2 * j + 1 + shift])

    each(0, cn, coarse_coeffs)

    for side in (0, 1):
        i, end = edge(side), side * (nx + 1)
        from_side("q", side, qe.at[end])
        from_side("c", side, c.at[end])
        from_side("n1p", side, n1h.at[side])
        more = c[i + 1] * qe[end]
        f0e[i] += more
        n1e[i + 1] += 0.5 * more
        n1e[end] = n1h[side] + 0.5 * c[end] * qe[i + 1]
        slow_step(i)

    send("n2r", n2r, rn2r, later, 1)

    def second(i):
        e = n1e[i + 1]
        f = c[i + 1] * (n1e[i] + n1e[i + 2] + inplane(e)) + react(e, t[i]) - n1r[i]
        t1e[i] = f
        n2e[i + 1] = e + 0.5 * f

    on_edges(lambda side, i, inner: second(i))
    own_edge = lambda ref: lambda side: ref.at[edge(side) + 1]
    to_sides("n2", own_edge(n2e), halo(n2e))
    to_later_sides("n2x", own_edge(n2e), slot(n2xh))
    each(1, nx - 1, second)
    send("n2e", n2e.at[pl.ds(1, nx)], rn2e, later, 1)

    def third(j, e_ref, r_ref, extra, missing=None):
        sums = [0.0, 0.0, 0.0, 0.0]
        for row in (0, 1):
            i = 2 * j + row
            e, r = e_ref[i + 1], r_ref[i]
            if missing == 0 and row == 0:
                x = e_ref[i + 2]
            elif missing == 1 and row == 1:
                x = e_ref[i]
            else:
                x = e_ref[i] + e_ref[i + 2]
            fe = c[i + 1] * (x + inplane(e)) + react(e, t[i]) - r
            fr = k[i] * (e - 0.5 * r)
            a, b, g, h = extra(i)
            sums[0] += a - W24 * fe
            sums[1] += b - W24 * fr
            sums[2] += g + SIXTH * fe
            sums[3] += h + SIXTH * fr
        dE[j + 1] = 0.25 * pair(sums[0])
        dR[j] = 0.25 * pair(sums[1])
        jE[j] = 0.25 * pair(sums[2])
        jR[j] = 0.25 * pair(sums[3])

    def extra_first(i):
        a, b, g, h = f0e[i], t1e[i], f0r[i], t1r[i]
        return (
            8 * W24 * b - 7 * W24 * a,
            8 * W24 * h - 7 * W24 * g,
            SIXTH * b - 2 * SIXTH * a,
            SIXTH * h - 2 * SIXTH * g,
        )

    for side in (0, 1):
        third(side * (cn - 1), n2e, n2r, extra_first, side)
        ds[side] = fold(dE[side * (cn - 1) + 1])
    to_sides("dp", slot(ds), slot(dh))
    each(1, cn - 1, lambda j: third(j, n2e, n2r, extra_first))

    for side in (0, 1):
        i, j, end = edge(side), side * (cn - 1), side * (nx + 1)
        from_side("n2", side, n2e.at[end])
        from_side("dp", side, dh.at[side])
        more = 0.25 * pair(c[i + 1] * n2e[end])
        dE[j + 1] -= W24 * more
        jE[j] += SIXTH * more
        dE[side * (cn + 1)] = unfold(dh[side]) - (0.25 * W24) * pair(c[end] * n2e[i + 1])

    def coarse_step(j, node, x):
        d, dr = dE[j + 1], dR[j]
        lap = 0.25 * (x + near(d, 0, 2)) + near(d, 1, 1) - 3.0 * d
        b = 0.25 * pair(node[2 * j + 1] + node[2 * j + 2])
        return 0.5 * (cc[j] * lap + react(b + d, tc[j]) - react(b, tc[j]) - dr)

    def coarse_slow(j):
        return jR[j] + 0.5 * kc[j] * (dE[j + 1] - 0.5 * dR[j])

    def coarse_first(j):
        e = jE[j] + coarse_step(j, n1e, dE[j] + dE[j + 2])
        r = coarse_slow(j)
        jE[j], jR[j] = e, r
        jts[j] = jnp.where(even_rows(e), e, r)

    each(0, 2, lambda side: coarse_first(side * (cn - 1)))
    for side in (0, 1):
        js[side] = fold(jE[side * (cn - 1)])
    to_sides("j", slot(js), slot(jh))
    to_later_sides("jx", slot(js), slot(jxh))
    each(1, cn - 1, coarse_first)
    send("jt", jts, jth, later, 1)

    def correct(j):
        for row in (0, 1):
            i = 2 * j + row
            u1e[i + 1] = n1e[i + 1] + dE[j + 1]
            u2e[i + 1] = n2e[i + 1] + jE[j]

    each(0, cn, correct)
    for side in (0, 1):
        end = side * (nx + 1)
        u1e[end] = n1e[end] + dE[side * (cn + 1)]
        u2e[end] = zeros

    def old_terms(j):
        for row in (0, 1):
            i = 2 * j + row
            u1, u2 = u1e[i + 1], u2e[i + 1]
            u1r, u2r = n1r[i] + dR[j], n2r[i] + jR[j]
            a1 = c[i + 1] * (u1e[i] + u1e[i + 2] + inplane(u1)) + react(u1, t[i]) - u1r
            a2 = c[i + 1] * (u2e[i] + u2e[i + 2] + inplane(u2)) + react(u2, t[i]) - u2r
            b1 = k[i] * (u1 - 0.5 * u1r)
            b2 = k[i] * (u2 - 0.5 * u2r)
            a0, b0 = f0e[i], f0r[i]
            s1e[i] = 8 * W24 * a1 - 7 * W24 * a0 - W24 * a2
            s1r[i] = 8 * W24 * b1 - 7 * W24 * b0 - W24 * b2
            s2e[i] = 5 * W24 * a2 - W24 * a0 - 4 * W24 * a1
            s2r[i] = 5 * W24 * b2 - W24 * b0 - 4 * W24 * b1

    each(0, cn, old_terms)

    for side in (0, 1):
        i, end = edge(side), side * (nx + 1)
        from_side("j", side, jh.at[side])
        more = c[i + 1] * (n2e[end] + unfold(jh[side]))
        s1e[i] -= W24 * more
        s2e[i] += 5 * W24 * more

    receive("n2r", rn2r, earlier)
    receive("n2e", rn2e, earlier)
    for side in (0, 1):
        from_side("n2x", side, n2xh.at[side], earlier)
        from_side("jx", side, jxh.at[side], earlier)
        end = side * (nx + 1)
        qne[end] = jnp.where(head, qe[end], n2xh[side] + unfold(jxh[side]))
    receive("jt", jth, earlier)

    def arrive(j):
        e, r = expand(jth[j])
        for row in (0, 1):
            i = 2 * j + row
            qne[i + 1] = jnp.where(head, qe[i + 1], rn2e[i] + e)
            qnr[i] = jnp.where(head, qr[i], rn2r[i] + r)

    each(0, cn, arrive)

    def next_first(i):
        e, r = qne[i + 1], qnr[i]
        f = c[i + 1] * (qne[i] + qne[i + 2] + inplane(e)) + react(e, t[i]) - r
        g = k[i] * (e - 0.5 * r)
        t0e[i], t0r[i] = f, g
        m1e[i + 1] = e + 0.5 * f + s1e[i]
        m1r[i] = r + 0.5 * g + s1r[i]

    on_edges(lambda side, i, inner: next_first(i))
    to_sides("m1", own_edge(m1e), halo(m1e))
    on_edges(lambda side, i, inner: next_first(inner - 1))

    def next_second(i, x):
        e, r = m1e[i + 1], m1r[i]
        f = c[i + 1] * (x + inplane(e)) + react(e, t[i]) - r
        g = k[i] * (e - 0.5 * r)
        t1e[i], t1r[i] = f, g
        m2 = e + 0.5 * f + s2e[i]
        m2e[i + 1] = m2
        m2r[i] = r + 0.5 * g + s2r[i]
        return m2

    def next_edge(side, i, inner):
        m2s[side] = next_second(i, m1e[inner])

    on_edges(next_edge)
    to_sides("m2p", slot(m2s), slot(m2h))
    each(2, nx - 2, next_first)
    each(1, nx - 1, lambda i: next_second(i, m1e[i] + m1e[i + 2]))

    for side in (0, 1):
        i, end = edge(side), side * (nx + 1)
        from_side("m1", side, m1e.at[end])
        from_side("m2p", side, m2h.at[side])
        more = c[i + 1] * m1e[end]
        t1e[i] += more
        m2e[i + 1] += 0.5 * more
        m2e[end] = m2h[side] + 0.5 * c[end] * m1e[i + 1]

    def extra_next(i):
        a, b, g, h = t0e[i], t1e[i], t0r[i], t1r[i]
        return (
            8 * W24 * b - 7 * W24 * a - s1e[i],
            8 * W24 * h - 7 * W24 * g - s1r[i],
            SIXTH * b - 2 * SIXTH * a - s1e[i] - s2e[i],
            SIXTH * h - 2 * SIXTH * g - s1r[i] - s2r[i],
        )

    each(0, 2, lambda side: third(side * (cn - 1), m2e, m2r, extra_next))
    for side in (0, 1):
        d2s[side] = fold(dE[side * (cn - 1) + 1])
    to_sides("d2", slot(d2s), slot(d2h))
    each(1, cn - 1, lambda j: third(j, m2e, m2r, extra_next))

    def final_slow(j):
        r = coarse_slow(j)
        for row in (0, 1):
            orr[2 * j + row] = m2r[2 * j + row] + r

    each(0, cn, final_slow)
    stores = [pltpu.make_async_copy(orr, out.at[0, 1], store_sem.at[0])]
    stores[-1].start()

    def final_fast(j):
        e = jE[j] + coarse_step(j, m1e, dE[j] + dE[j + 2])
        for row in (0, 1):
            oe[2 * j + row] = m2e[2 * j + 1 + row] + e

    each(1, cn - 1, final_fast)
    if cn > 2:
        inside = pl.ds(2, nx - 4)
        stores.append(pltpu.make_async_copy(oe.at[inside], out.at[0, 0, inside], store_sem.at[1]))
        stores[-1].start()

    for side in (0, 1):
        j = side * (cn - 1)
        inner = dE[2 + side * (cn - 3)]
        e = jE[j] + coarse_step(j, m1e, inner)
        oe[2 * j] = m2e[2 * j + 1] + e
        oe[2 * j + 1] = m2e[2 * j + 2] + e
    for side in (0, 1):
        j = side * (cn - 1)
        from_side("d2", side, d2h.at[side])
        e = 0.125 * cc[j] * unfold(d2h[side])
        oe[2 * j] += e
        oe[2 * j + 1] += e
        rows = pl.ds(2 * j, 2)
        stores.append(
            pltpu.make_async_copy(oe.at[rows], out.at[0, 0, rows], store_sem.at[2 + side])
        )
        stores[-1].start()

    for name, src, dst, when, dp, dside in pending:

        @pl.when(when)
        def _():
            copy_of(name, src, dst, dp, dside).wait_send()

    for store in stores:
        store.wait()


def per_device(start, conduct, threshold, recovery):
    nx, ny, nz = conduct.shape
    cn = nx // 2

    def planes(count, rows=ny):
        return pltpu.VMEM((count, rows, nz), jnp.float32)

    own, padded, coarse, two, half = (
        planes(nx), planes(nx + 2), planes(cn), planes(2), planes(2, ny // 2)
    )
    scratch = [
        padded, own, padded, own, own, coarse, coarse, coarse,
        own, own, padded, own, padded, own, own, own,
        planes(cn + 2), coarse, coarse, coarse, padded, padded, own, own, own, own,
        padded, own, padded, own, padded, own, own, own, own, own,
        two, two, half, half, half, half, half, two, own, own, coarse, coarse,
        two, two, half, half,
        pltpu.SemaphoreType.DMA((5,)),
        pltpu.SemaphoreType.DMA((4,)),
        pltpu.SemaphoreType.DMA((len(MESSAGES),)),
        pltpu.SemaphoreType.DMA((len(MESSAGES),)),
    ]
    return pl.pallas_call(
        kernel,
        out_shape=jax.ShapeDtypeStruct(start.shape, jnp.float32),
        in_specs=[pl.BlockSpec(memory_space=pl.ANY)] * 4,
        out_specs=pl.BlockSpec(memory_space=pl.ANY),
        scratch_shapes=scratch,
        compiler_params=pltpu.CompilerParams(
            collective_id=0, has_side_effects=True, vmem_limit_bytes=48 * 1024 * 1024
        ),
    )(start, conduct, threshold, recovery)


def solution(mesh):
    placed = (
        P("tm", None, "space", None, None),
        P("space", None, None),
        P("space", None, None),
        P("space", None, None),
    )
    return jax.shard_map(
        per_device,
        mesh=mesh,
        in_specs=placed,
        out_specs=P("tm", None, "space", None, None),
        check_vma=False,
    )
```

time: 98 us -> 29.4 us (0.30)
  the two profiles are of different devices: /device:TPU:28 before, /device:TPU:12 now
where the time goes in v1:
time: 29.4 us; the launch traced here: 29.2 us
  Pallas kernels  24.5 us (83%)
  local copies, waits for them, and re-layouts  4.69 us (16%)
    pallas_call x1, Pallas kernels, per_device(): pl.pallas_call(kernel, out_shape=jax.ShapeDtypeStruct(start.shape, jnp.fl...  24.5 us
    unnamed x9, local copies, waits for them, and re-layouts  4.69 us

profile of v1, /device:TPU:12, one launch (start us, length us, event | category | flops | bytes accessed | tf_op | source)
XLA Modules:
  0.0 29.2 jit_solution(13828737193706030490)
XLA Ops:
  0.0 0.0 copy-start
  0.0 1.0 %copy-done = f32[1,2,8,64,128]{4,3,2,1,0:T(8,128)S(1)} copy-done((f32[1,2,8,64,128]{4,3,2,1,0:T(8,128)S(1)}, f32[1,2,8,64,128]{4,3,2,1,0:T(8,128)}, u32[]{:S(2)}) %copy-start) | copy-done | bytes 524312
  1.0 0.0 copy-start.1
  1.0 0.9 %copy-done.1 = f32[8,64,128]{2,1,0:T(8,128)S(1)} copy-done((f32[8,64,128]{2,1,0:T(8,128)S(1)}, f32[8,64,128]{2,1,0:T(8,128)}, u32[]{:S(2)}) %copy-start.1) | copy-done | bytes 262168
  2.0 0.0 copy-start.2
  2.0 0.9 %copy-done.2 = f32[8,64,128]{2,1,0:T(8,128)S(1)} copy-done((f32[8,64,128]{2,1,0:T(8,128)S(1)}, f32[8,64,128]{2,1,0:T(8,128)}, u32[]{:S(2)}) %copy-start.2) | copy-done | bytes 262168
  2.9 0.0 copy-start.3
  2.9 0.9 %copy-done.3 = f32[8,64,128]{2,1,0:T(8,128)S(1)} copy-done((f32[8,64,128]{2,1,0:T(8,128)S(1)}, f32[8,64,128]{2,1,0:T(8,128)}, u32[]{:S(2)}) %copy-start.3) | copy-done | bytes 262168
  3.9 24.5 %shard_map.46 = f32[1,2,8,64,128]{4,3,2,1,0:T(8,128)S(1)} custom-call(f32[1,2,8,64,128]{4,3,2,1,0:T(8,128)S(1)} %copy-done, f32[8,64,128]{2,1,0:T(8,128)S(1)} %copy-done.1, f32[8,64,128]{2,1,0:T(8,128)S(1)} %copy-done.2, f32[8,64,128]{2,1,0:T(8,128)S(1)} %copy-done.3), custom_call_target="tpu_custom_call" | custom-call | tf_op jit(solution)/shard_map/pallas_call | solution.py:502
  28.4 0.8 %copy.6 = f32[1,2,8,64,128]{4,3,2,1,0:T(8,128)} copy(f32[1,2,8,64,128]{4,3,2,1,0:T(8,128)S(1)} %shard_map.46) | data formatting | bytes 1048576
Async XLA Ops:
  0.0 1.0 %copy-start = (f32[1,2,8,64,128]{4,3,2,1,0:T(8,128)S(1)}, f32[1,2,8,64,128]{4,3,2,1,0:T(8,128)}, u32[]{:S(2)}) copy-start(f32[1,2,8,64,128]{4,3,2,1,0:T(8,128)} %start.1) | copy-start | bytes 1572868
  1.0 0.9 %copy-start.1 = (f32[8,64,128]{2,1,0:T(8,128)S(1)}, f32[8,64,128]{2,1,0:T(8,128)}, u32[]{:S(2)}) copy-start(f32[8,64,128]{2,1,0:T(8,128)} %cond.1) | copy-start | bytes 786436
  2.0 0.9 %copy-start.2 = (f32[8,64,128]{2,1,0:T(8,128)S(1)}, f32[8,64,128]{2,1,0:T(8,128)}, u32[]{:S(2)}) copy-start(f32[8,64,128]{2,1,0:T(8,128)} %thr.1) | copy-start | bytes 786436
  2.9 0.9 %copy-start.3 = (f32[8,64,128]{2,1,0:T(8,128)S(1)}, f32[8,64,128]{2,1,0:T(8,128)}, u32[]{:S(2)}) copy-start(f32[8,64,128]{2,1,0:T(8,128)} %rec.1) | copy-start | bytes 786436
